TPU v7x, 32 devices: a whole 2x2x4 slice. The times are simulated.
32 devices in a mesh: ctx: 8 (over z, x), ts: 4 (over y, core).
Axes of the slice: x: 2, y: 2, z: 4, core: 2. Of those that a mesh axis runs over, the one named last changes fastest.
Arguments:
- se_input: bfloat16 [2048, 3, 4096], P('ctx', None, 'ts'), may hold values from -6 to 6
- mr_input: bfloat16 [2048, 2, 4096], P('ctx', None, 'ts'), may hold values from -6 to 6
- cotangent: bfloat16 [2048, 4096], P('ctx', 'ts'), may hold values from -6 to 6
- se_featurizer: float32 [3, 3, 4096], P(None, None, 'ts'), may hold values from -3.5 to 3.5
- mr_featurizer: float32 [3, 3, 4096], P(None, None, 'ts'), may hold values from -3.5 to 3.5
- se_filter: float32 [7, 4096], P(None, 'ts'), may hold values from -2 to 2
- mr_filter: float32 [128, 4096], P(None, 'ts'), may hold values from -1 to 1
- decay_rate: float32 [4096], P('ts'), may hold values from 0.003 to 0.05
Outputs:
- grad_se_input: bfloat16 [2048, 3, 4096], P('ctx', None, 'ts')
- grad_mr_input: bfloat16 [2048, 2, 4096], P('ctx', None, 'ts')
- grad_se_filter: float32 [7, 4096], P(None, 'ts')
- grad_mr_filter: float32 [128, 4096], P(None, 'ts')
All inputs are finite; a program needn't handle non-finite values.
Results may differ from a plain program's by a relative error of at most 0.0061.
Values may be sent and summed in bfloat16 or wider, within the bound.
A program may use at most 128 MiB of HBM per device.

v0:
```python
import functools
import math

import jax
import jax.numpy as jnp
import numpy as np
from jax import lax
from jax.experimental import pallas as pl
from jax.experimental.pallas import tpu as pltpu
from jax.sharding import PartitionSpec as P

F32 = jnp.float32
BF16 = jnp.bfloat16
EDGE = 16
PAD = 8


def round_up(value, unit):
    return -(-value // unit) * unit


def transforms(rows, taps):
    behind = taps
    span = behind + rows + EDGE
    n = round_up(span, 32)
    half = n // 2
    freq = 2.0 * np.pi * (np.arange(half) + 0.5) / n

    def forward(at):
        angle = freq[:, None] * at[None, :]
        return np.concatenate([np.cos(angle), -np.sin(angle)], axis=0)

    def inverse(at):
        angle = at[:, None] * freq[None, :]
        return np.concatenate([np.cos(angle), -np.sin(angle)], axis=1) * (2.0 / n)

    ahead = forward(np.arange(n)).astype(np.float32)
    ahead_high = ahead.astype(jnp.bfloat16)
    ahead_low = (ahead - ahead_high.astype(np.float32)).astype(jnp.bfloat16)[:, :taps]
    mixed = inverse(np.arange(rows + EDGE) + behind).astype(jnp.bfloat16)
    back = inverse(np.arange(rows + EDGE)).astype(jnp.bfloat16)
    lags = inverse(np.arange(taps) - behind).astype(jnp.bfloat16)
    return n, ahead_high, ahead_low, mixed, back, lags


def chunks(start, stop, size):
    return [(at, min(size, stop - at)) for at in range(start, stop, size)]


def body(
    n_ctx, length, taps, short, feat, group,
    se, mr, cot, sef, mrf, sfilt, mfilt, decay, ahead, ahead_low, inv_mixed, inv_back, inv_lags,
    out_se, out_mr, out_short, out_medium,
    se_behind, mr_behind, se_after, mr_after, cot_after,
    win, y1, q1, k1, v1, pse, z1, k2, v2, z2,
    hist, up, kspec, gspec, xspec, damp,
    dwide, d2, dz1, d1,
    dks, rs, ag, sks, srs, sag,
    edge_send, edge_recv, hist_send, hist_recv, up_send, up_recv,
    rs_send, rs_recv, ag_send, ag_recv, srs_send, srs_recv, sag_send, sag_recv,
):
    rows, channels = cot.shape
    half = length // 2
    groups = channels // group
    lane_blocks = min(n_ctx, 8)
    row_blocks = n_ctx // lane_blocks
    lane_width = channels // lane_blocks
    piece_rows = taps // row_blocks
    per_group = group // lane_width
    end = rows + EDGE
    up_rows = taps + EDGE
    me = lax.axis_index("ctx")
    has_behind = me > 0
    has_after = me < n_ctx - 1

    barrier = pltpu.get_barrier_semaphore()

    def greet(step, carry):
        pl.semaphore_signal(
            barrier, inc=1, device_id={"ctx": lax.rem(me + step, n_ctx)},
            device_id_type=pl.DeviceIdType.MESH,
        )
        return carry

    lax.fori_loop(1, n_ctx, greet, 0)
    pl.semaphore_wait(barrier, n_ctx - 1)

    def remote(src, dst, send, recv, to):
        return pltpu.make_async_remote_copy(
            src_ref=src, dst_ref=dst, send_sem=send, recv_sem=recv,
            device_id={"ctx": to}, device_id_type=pl.DeviceIdType.MESH,
        )

    last = pl.ds(rows - EDGE, EDGE)
    first = pl.ds(0, EDGE)

    def to_after():
        to = me + 1
        return [
            remote(se.at[:, last, :], se_behind, edge_send.at[0], edge_recv.at[0], to),
            remote(mr.at[:, last, :], mr_behind, edge_send.at[1], edge_recv.at[1], to),
        ]

    def to_behind():
        to = me - 1
        return [
            remote(se.at[:, first, :], se_after, edge_send.at[2], edge_recv.at[2], to),
            remote(mr.at[1, first, :], mr_after, edge_send.at[3], edge_recv.at[3], to),
            remote(cot.at[first, :], cot_after, edge_send.at[4], edge_recv.at[4], to),
        ]

    def hist_copy(i):
        cols = pl.ds(pl.multiple_of(i * group, group), group)
        return remote(
            hist.at[pl.ds(rows, taps), cols], hist.at[pl.ds(0, taps), cols],
            hist_send.at[i], hist_recv.at[i], me + 1,
        )

    def up_copy(i):
        cols = pl.ds(pl.multiple_of(i * group, group), group)
        return remote(
            up.at[pl.ds(0, up_rows), cols], up.at[pl.ds(rows, up_rows), cols],
            up_send.at[i], up_recv.at[i], me - 1,
        )

    @pl.when(has_after)
    def _():
        for copy in to_after():
            copy.start()

    @pl.when(has_behind)
    def _():
        for copy in to_behind():
            copy.start()

    @pl.when(jnp.logical_not(has_behind))
    def _():
        se_behind[...] = jnp.zeros_like(se_behind)
        mr_behind[...] = jnp.zeros_like(mr_behind)
        hist[0:taps, :] = jnp.zeros((taps, channels), BF16)

    @pl.when(jnp.logical_not(has_after))
    def _():
        se_after[...] = jnp.zeros_like(se_after)
        mr_after[...] = jnp.zeros_like(mr_after)
        cot_after[...] = jnp.zeros_like(cot_after)
        up[rows : rows + up_rows, :] = jnp.zeros((up_rows, channels), BF16)

    spare = length - (taps + rows + EDGE)
    if spare:
        hist[length - spare :, :] = jnp.zeros((spare, channels), BF16)
        up[length - spare :, :] = jnp.zeros((spare, channels), BF16)
    win[:, 0:PAD, :] = jnp.zeros((5, PAD, group), F32)
    y1[0:PAD, :] = jnp.zeros((PAD, group), F32)
    pse[0:PAD, :] = jnp.zeros((PAD, channels), F32)
    d2[:, end:, :] = jnp.zeros((3, d2.shape[1] - end, group), F32)
    dz1[end:, :] = jnp.zeros((dz1.shape[0] - end, group), F32)
    sks[...] = jnp.zeros_like(sks)

    def spectra(i, carry):
        cols = pl.ds(pl.multiple_of(i * group, group), group)
        lag = lax.broadcasted_iota(jnp.int32, (taps, group), 0).astype(F32)
        damping = jnp.exp(-lag * decay[:, cols])
        damp[:, cols] = damping
        kernel = mfilt[:, cols] * damping
        high = kernel.astype(BF16)
        low = (kernel - high.astype(F32)).astype(BF16)
        table = ahead[:, 0:taps]
        kspec[:, cols] = (
            jnp.dot(table, high, preferred_element_type=F32)
            + jnp.dot(table, low, preferred_element_type=F32)
            + jnp.dot(ahead_low[...], high, preferred_element_type=F32)
        )
        return carry

    lax.fori_loop(0, groups, spectra, 0)

    @pl.when(has_behind)
    def _():
        for copy in to_after():
            copy.wait_recv()

    @pl.when(has_after)
    def _():
        for copy in to_behind():
            copy.wait_recv()

    def forward(i, carry):
        cols = pl.ds(pl.multiple_of(i * group, group), group)
        for part in range(3):
            win[part, PAD : PAD + EDGE, :] = se_behind[part, :, cols].astype(F32)
            win[part, PAD + EDGE : PAD + EDGE + rows, :] = se[part, :, cols].astype(F32)
            win[part, PAD + EDGE + rows :, :] = se_after[part, :, cols].astype(F32)
        for part in range(2):
            win[3 + part, PAD : PAD + EDGE, :] = mr_behind[part, :, cols].astype(F32)
            win[3 + part, PAD + EDGE : PAD + EDGE + rows, :] = mr[part, :, cols].astype(F32)
        win[4, PAD + EDGE + rows :, :] = mr_after[:, cols].astype(F32)

        def se_mix(part, at, size):
            return sum(
                sef[3 * j + part : 3 * j + part + 1, cols] * win[part, pl.ds(PAD + at - j, size), :]
                for j in range(feat)
            )

        for at, size in [(0, EDGE)] + chunks(EDGE, EDGE + end, 32):
            here = pl.ds(PAD + at, size)
            q = se_mix(0, at, size)
            k = se_mix(1, at, size)
            v = se_mix(2, at, size)
            q1[here, cols] = q
            k1[here, cols] = k
            v1[here, cols] = v
            pse[here, cols] = (k * v).astype(BF16).astype(F32)
            z = sum(
                sfilt[j : j + 1, cols] * pse[pl.ds(PAD + at - j, size), cols] for j in range(short)
            )
            z1[here, cols] = z
            y1[here, :] = (q * z).astype(BF16).astype(F32)
            if at < EDGE:
                continue

            def mr_mix(part):
                return sum(
                    mrf[3 * j + part : 3 * j + part + 1, cols]
                    * (
                        y1[pl.ds(PAD + at - j, size), :]
                        if part == 2
                        else win[3 + part, pl.ds(PAD + at - j, size), :]
                    )
                    for j in range(feat)
                )

            k = mr_mix(1)
            v = mr_mix(2)
            k2[here, cols] = k
            v2[here, cols] = v
            t = at - EDGE
            hist[pl.ds(taps + t, size), cols] = (k * v).astype(BF16)
            if t < rows:
                up[pl.ds(t, size), cols] = (cot[pl.ds(t, size), cols].astype(F32) * mr_mix(0)).astype(BF16)

        @pl.when(has_after)
        def _():
            hist_copy(i).start()

        @pl.when(has_behind)
        def _():
            up_copy(i).start()

        gspec[:, cols] = jnp.dot(ahead[:, 0:rows], up[0:rows, cols], preferred_element_type=F32)
        xspec[:, cols] = jnp.dot(
            ahead[:, taps:length], hist[taps:length, cols], preferred_element_type=F32
        )
        return carry

    lax.fori_loop(0, groups, forward, 0)

    def piece_of(d):
        at_rows = pl.ds(pl.multiple_of((d // lane_blocks) * piece_rows, 16), piece_rows)
        at_cols = pl.ds(pl.multiple_of(lax.rem(d, lane_blocks) * lane_width, lane_width), lane_width)
        return at_rows, at_cols

    def rs_copy(to, slot):
        at_rows, at_cols = piece_of(to)
        return remote(dks.at[at_rows, at_cols], rs.at[slot], rs_send.at[to], rs_recv.at[slot], to)

    def ag_copy(to, slot):
        return remote(ag.at[slot], ag.at[slot], ag_send.at[to], ag_recv.at[slot], to)

    def srs_copy(to, slot):
        _, at_cols = piece_of(to)
        return remote(sks.at[:, at_cols], srs.at[slot], srs_send.at[to], srs_recv.at[slot], to)

    def sag_copy(to, slot):
        return remote(sag.at[slot], sag.at[slot], sag_send.at[to], sag_recv.at[slot], to)

    def for_peers(act):
        def step(s, carry):
            act(lax.rem(me + s, n_ctx))
            return carry

        lax.fori_loop(1, n_ctx, step, 0)

    def medium(i, carry):
        cols = pl.ds(pl.multiple_of(i * group, group), group)

        @pl.when(has_behind)
        def _():
            hist_copy(i).wait_recv()

        x = xspec[:, cols] + jnp.dot(ahead[:, 0:taps], hist[0:taps, cols], preferred_element_type=F32)
        xr, xi = x[:half], x[half:]
        gr, gi = gspec[0:half, cols], gspec[half:, cols]
        lag = jnp.concatenate(
            [(gr * xr + gi * xi).astype(BF16), (gi * xr - gr * xi).astype(BF16)], axis=0
        )
        dks[:, cols] = jnp.dot(inv_lags[...], lag, preferred_element_type=F32).astype(BF16)

        for block in range(per_group):
            for row_block in range(row_blocks):
                owner = row_block * lane_blocks + i * per_group + block

                @pl.when(owner != me)
                def _():
                    rs_copy(owner, me).start()

        kr, ki = kspec[0:half, cols], kspec[half:, cols]
        y = jnp.concatenate(
            [(xr * kr - xi * ki).astype(BF16), (xr * ki + xi * kr).astype(BF16)], axis=0
        )
        z2[:, cols] = jnp.dot(inv_mixed[...], y, preferred_element_type=F32)
        return carry

    lax.fori_loop(0, groups, medium, 0)

    inside = jnp.where(has_after, 1.0, 0.0).astype(F32)

    def backward(i, carry):
        cols = pl.ds(pl.multiple_of(i * group, group), group)

        @pl.when(has_after)
        def _():
            up_copy(i).wait_recv()

        d = gspec[:, cols] + jnp.dot(
            ahead[:, rows:length], up[rows:length, cols], preferred_element_type=F32
        )
        dr, di = d[:half], d[half:]
        kr, ki = kspec[0:half, cols], kspec[half:, cols]
        y = jnp.concatenate(
            [(dr * kr + di * ki).astype(BF16), (di * kr - dr * ki).astype(BF16)], axis=0
        )
        dwide[...] = jnp.dot(inv_back[...], y, preferred_element_type=F32)

        for t, size in chunks(0, end, 32):
            here = pl.ds(t, size)
            there = pl.ds(PAD + EDGE + t, size)
            w = dwide[here, :]
            if t >= rows:
                w = w * inside
                g = cot_after[:, cols].astype(F32)
            else:
                g = cot[here, cols].astype(F32)
            d2[0, here, :] = g * z2[here, cols]
            d2[1, here, :] = w * v2[there, cols]
            d2[2, here, :] = w * k2[there, cols]

        def mr_back(part, t, size):
            return sum(
                mrf[3 * j + part : 3 * j + part + 1, cols] * d2[part, pl.ds(t + j, size), :]
                for j in range(feat)
            )

        for t, size in chunks(0, end, 32):
            here = pl.ds(t, size)
            there = pl.ds(PAD + EDGE + t, size)
            dy = mr_back(2, t, size)
            d1[0, here, :] = dy * z1[there, cols]
            dz1[here, :] = dy * q1[there, cols]
            if t < rows:
                out_mr[0, here, cols] = mr_back(0, t, size).astype(BF16)
                out_mr[1, here, cols] = mr_back(1, t, size).astype(BF16)

        sums = [jnp.zeros((8, group), F32) for _ in range(short)]
        for t, size in chunks(0, end, 32):
            here = pl.ds(t, size)
            there = pl.ds(PAD + EDGE + t, size)
            w = sum(sfilt[j : j + 1, cols] * dz1[pl.ds(t + j, size), :] for j in range(short))
            d1[1, here, :] = w * v1[there, cols]
            d1[2, here, :] = w * k1[there, cols]
            if t < rows:
                dz = dz1[here, :]
                for j in range(short):
                    term = dz * pse[pl.ds(PAD + EDGE + t - j, size), cols]
                    for s in range(0, size, 8):
                        sums[j] = sums[j] + term[s : s + 8]
        for j in range(short):
            sks[j : j + 1, cols] = jnp.sum(sums[j], axis=0, keepdims=True)

        for t, size in chunks(0, rows, 32):
            here = pl.ds(t, size)
            for part in range(3):
                out_se[part, here, cols] = sum(
                    sef[3 * j + part : 3 * j + part + 1, cols] * d1[part, pl.ds(t + j, size), :]
                    for j in range(feat)
                ).astype(BF16)

        @pl.when(i == max(groups - 2, 0))
        def _():
            at_rows, at_cols = piece_of(me)
            rs[me] = dks[at_rows, at_cols]
            for_peers(lambda d: rs_copy(d, d).wait_recv())
            total = rs[0].astype(F32)
            for d in range(1, n_ctx):
                total = total + rs[d].astype(F32)
            ag[me] = total.astype(BF16)
            for_peers(lambda d: ag_copy(d, me).start())

        return carry

    lax.fori_loop(0, groups, backward, 0)

    _, my_cols = piece_of(me)
    for_peers(lambda d: srs_copy(d, me).start())
    srs[me] = sks[:, my_cols]
    scale = 1.0 / math.sqrt(rows * n_ctx)
    for_peers(lambda d: ag_copy(d, d).wait_recv())
    for d in range(n_ctx):
        r, c = (d // lane_blocks) * piece_rows, (d % lane_blocks) * lane_width
        out_medium[r : r + piece_rows, c : c + lane_width] = (
            ag[d].astype(F32) * damp[r : r + piece_rows, c : c + lane_width] * scale
        )
    for_peers(lambda d: srs_copy(d, d).wait_recv())
    total = srs[0]
    for d in range(1, n_ctx):
        total = total + srs[d]
    sag[me] = total * scale
    for_peers(lambda d: sag_copy(d, me).start())

    @pl.when(has_after)
    def _():
        for copy in to_after():
            copy.wait_send()
        for i in range(groups):
            hist_copy(i).wait_send()

    @pl.when(has_behind)
    def _():
        for copy in to_behind():
            copy.wait_send()
        for i in range(groups):
            up_copy(i).wait_send()

    for_peers(lambda d: rs_copy(d, me).wait_send())
    for_peers(lambda d: ag_copy(d, me).wait_send())
    for_peers(lambda d: srs_copy(d, me).wait_send())
    for_peers(lambda d: sag_copy(d, d).wait_recv())
    for d in range(lane_blocks):
        c = d * lane_width
        out_short[:, c : c + lane_width] = sag[d][0:short]
    for_peers(lambda d: sag_copy(d, me).wait_send())


def local(n_ctx, se_input, mr_input, cotangent, se_featurizer, mr_featurizer, se_filter, mr_filter, decay_rate):
    rows, channels = cotangent.shape
    taps, short, feat = mr_filter.shape[0], se_filter.shape[0], se_featurizer.shape[0]
    group = min(256, channels)
    groups = channels // group
    length, ahead, ahead_low, inv_mixed, inv_back, inv_lags = transforms(rows, taps)
    lane_blocks = min(n_ctx, 8)
    lane_width = channels // lane_blocks
    piece_rows = taps // (n_ctx // lane_blocks)
    wide = PAD + EDGE + rows + EDGE
    end = rows + EDGE
    vmem = pltpu.VMEM
    dma = pltpu.SemaphoreType.DMA
    scratch = (
        [vmem((3, EDGE, channels), BF16), vmem((2, EDGE, channels), BF16)]
        + [vmem((3, EDGE, channels), BF16), vmem((EDGE, channels), BF16), vmem((EDGE, channels), BF16)]
        + [vmem((5, wide, group), F32), vmem((wide, group), F32)]
        + [vmem((wide, channels), F32)] * 7
        + [vmem((end, channels), F32)]
        + [vmem((length, channels), BF16)] * 2
        + [vmem((length, channels), F32)] * 3
        + [vmem((taps, channels), F32)]
        + [vmem((end, group), F32), vmem((3, end + 16, group), F32)]
        + [vmem((end + 16, group), F32), vmem((3, end + 16, group), F32)]
        + [vmem((taps, channels), BF16)]
        + [vmem((n_ctx, piece_rows, lane_width), BF16)] * 2
        + [vmem((8, channels), F32)]
        + [vmem((n_ctx, 8, lane_width), F32)] * 2
        + [dma((5,))] * 2
        + [dma((groups,))] * 4
        + [dma((n_ctx,))] * 8
    )
    out_se, out_mr, out_short, out_medium = pl.pallas_call(
        functools.partial(body, n_ctx, length, taps, short, feat, group),
        out_shape=(
            jax.ShapeDtypeStruct((3, rows, channels), BF16),
            jax.ShapeDtypeStruct((2, rows, channels), BF16),
            jax.ShapeDtypeStruct((short, channels), F32),
            jax.ShapeDtypeStruct((taps, channels), F32),
        ),
        in_specs=[pl.BlockSpec(memory_space=pltpu.VMEM)] * 13,
        out_specs=[pl.BlockSpec(memory_space=pltpu.VMEM)] * 4,
        scratch_shapes=scratch,
        compiler_params=pltpu.CompilerParams(
            collective_id=0, has_side_effects=True, vmem_limit_bytes=56 * 1024 * 1024
        ),
        cost_estimate=pl.CostEstimate(
            flops=12 * length * length * channels, bytes_accessed=14 * rows * channels * 2, transcendentals=0
        ),
        name="hyena_pair",
    )(
        jnp.transpose(se_input, (1, 0, 2)),
        jnp.transpose(mr_input, (1, 0, 2)),
        cotangent,
        se_featurizer.reshape(3 * feat, channels),
        mr_featurizer.reshape(3 * feat, channels),
        se_filter,
        mr_filter,
        decay_rate[None, :],
        ahead, ahead_low, inv_mixed, inv_back, inv_lags,
    )
    return jnp.transpose(out_se, (1, 0, 2)), jnp.transpose(out_mr, (1, 0, 2)), out_short, out_medium


def solution(mesh):
    placed = (
        P("ctx", None, "ts"),
        P("ctx", None, "ts"),
        P("ctx", "ts"),
        P(None, None, "ts"),
        P(None, None, "ts"),
        P(None, "ts"),
        P(None, "ts"),
        P("ts"),
    )
    return jax.shard_map(
        functools.partial(local, mesh.shape["ctx"]),
        mesh=mesh,
        in_specs=placed,
        out_specs=(P("ctx", None, "ts"), P("ctx", None, "ts"), P(None, "ts"), P(None, "ts")),
        check_vma=False,
    )
```

profile of v0, /device:TPU:0, one launch (start us, length us, event | category | flops | bytes accessed | tf_op | source)
XLA Modules:
  0.0 65.2 jit_solution(4458517971267990296)
XLA Ops:
  0.6 1.4 %reshape.14.sef = f32[9,1024]{1,0:T(8,128)} reshape(f32[3,3,1024]{2,1,0:T(4,128)} %param.16) | data formatting | bytes 73728 | tf_op jit(solution)/shard_map/reshape | solution.py:498
  2.1 1.4 %reshape.15.mrf = f32[9,1024]{1,0:T(8,128)} reshape(f32[3,3,1024]{2,1,0:T(4,128)} %param.17) | data formatting | bytes 73728 | tf_op jit(solution)/shard_map/reshape | solution.py:499
  3.5 2.5 %copy.20 = bf16[256,2,1024]{2,0,1:T(8,128)(2,1)} copy(bf16[256,2,1024]{2,1,0:T(2,128)(2,1)} %param.14) | data formatting | bytes 2097152 | tf_op args[1]
  6.0 53.2 %hyena_pair.1 = (bf16[3,256,1024]{2,1,0:T(8,128)(2,1)}, bf16[2,256,1024]{2,1,0:T(8,128)(2,1)}, f32[7,1024]{1,0:T(8,128)}, f32[128,1024]{1,0:T(8,128)}) custom-call(bf16[3,256,1024]{2,1,0:T(8,128)(2,1)} %bitcast.10, bf16[2,256,1024]{2,1,0:T(8,128)(2,1)} %bitcast.9, bf16[256,1024]{1,0:T(8,128)(2,1)} %cot.1, f32[9,1024]{1,0:T(8,128)} %reshape.14.sef, ...), custom_call_target="tpu_custom_call" | custom-call | flops 2126512128 | bytes 7340032 | tf_op jit(solution)/shard_map/hyena_pair/pallas_call | solution.py:476
  59.2 0.0 copy-start
  59.2 3.4 %copy.18 = bf16[256,2,1024]{2,1,0:T(2,128)(2,1)} copy(bf16[256,2,1024]{2,0,1:T(8,128)(2,1)} %bitcast.8) | data formatting | bytes 2097152
  62.6 0.0 copy-done
  62.6 0.0 copy-start.2
  62.6 0.0 copy-start.1
  62.6 1.1 %copy.24 = bf16[256,3,1024]{2,0,1:T(8,128)(2,1)} copy(bf16[256,3,1024]{2,0,1:T(8,128)(2,1)S(1)} %bitcast.7) | data formatting | bytes 3145728
  63.8 0.0 copy-done.2
  63.8 0.6 copy.25
  64.4 0.0 copy-done.1
  64.4 0.8 %copy.26 = f32[128,1024]{1,0:T(8,128)} copy(f32[128,1024]{1,0:T(8,128)S(1)} %copy-done.1) | data formatting | bytes 1048576
Async XLA Ops:
  59.2 3.4 %copy-start = (bf16[3,256,1024]{2,1,0:T(8,128)(2,1)S(1)}, bf16[3,256,1024]{2,1,0:T(8,128)(2,1)}, u32[]{:S(2)}) copy-start(bf16[3,256,1024]{2,1,0:T(8,128)(2,1)} %get-tuple-element.8) | copy-start | bytes 4718596
  62.6 1.1 %copy-start.2 = (f32[7,1024]{1,0:T(8,128)S(1)}, f32[7,1024]{1,0:T(8,128)}, u32[]{:S(2)}) copy-start(f32[7,1024]{1,0:T(8,128)} %get-tuple-element.22) | copy-start | bytes 86020
  62.6 1.8 %copy-start.1 = (f32[128,1024]{1,0:T(8,128)S(1)}, f32[128,1024]{1,0:T(8,128)}, u32[]{:S(2)}) copy-start(f32[128,1024]{1,0:T(8,128)} %get-tuple-element.23) | copy-start | bytes 1572868
where the time goes:
time: 65.5 us; the launch traced here: 65.2 us
  Pallas kernels  53.2 us (81%)
  local copies, waits for them, and re-layouts  11.3 us (17%)
    pallas_call x1, Pallas kernels, local(): pl.pallas_call(functools.partial(body, n_ctx, length, taps, short, feat,...  53.2 us
    unnamed x11, local copies, waits for them, and re-layouts  8.42 us
    reshape x1, local copies, waits for them, and re-layouts, local(): se_featurizer.reshape(3 * feat, channels)  1.45 us
    reshape x1, local copies, waits for them, and re-layouts, local(): mr_featurizer.reshape(3 * feat, channels)  1.45 us

commit v1 on v0

--- a/solution.py
+++ b/solution.py
@@ -12,7 +12,8 @@
 F32 = jnp.float32
 BF16 = jnp.bfloat16
 EDGE = 16
-PAD = 8
+NEAR = 16
+FAR = 48
 
 
 def round_up(value, unit):
@@ -37,10 +38,18 @@
     ahead = forward(np.arange(n)).astype(np.float32)
     ahead_high = ahead.astype(jnp.bfloat16)
     ahead_low = (ahead - ahead_high.astype(np.float32)).astype(jnp.bfloat16)[:, :taps]
-    mixed = inverse(np.arange(rows + EDGE) + behind).astype(jnp.bfloat16)
-    back = inverse(np.arange(rows + EDGE)).astype(jnp.bfloat16)
+    wide = rows + 2 * EDGE
+    place = (np.arange(wide) % 8) * (wide // 8) + np.arange(wide) // 8
+    weave = (place[:, None] == np.arange(wide)[None, :]).astype(jnp.bfloat16)
+    unweave = np.ascontiguousarray(weave.T[EDGE : EDGE + rows])
+    at = place - EDGE
+    from_hist = np.where(at >= 0, ahead[:, np.maximum(behind + at, 0)], 0.0).astype(jnp.bfloat16)
+    own = (at >= 0) & (at < rows)
+    from_up = np.where(own, ahead[:, np.clip(at, 0, rows)], 0.0).astype(jnp.bfloat16)
+    mixed = inverse(at + behind).astype(jnp.bfloat16)
+    back = inverse(at).astype(jnp.bfloat16)
     lags = inverse(np.arange(taps) - behind).astype(jnp.bfloat16)
-    return n, ahead_high, ahead_low, mixed, back, lags
+    return n, (ahead_high, ahead_low, from_hist, from_up, mixed, back, lags, weave, unweave)
 
 
 def chunks(start, stop, size):
@@ -49,11 +58,11 @@
 
 def body(
     n_ctx, length, taps, short, feat, group,
-    se, mr, cot, sef, mrf, sfilt, mfilt, decay, ahead, ahead_low, inv_mixed, inv_back, inv_lags,
+    se, mr, cot, sef, mrf, sfilt, mfilt, decay, ahead, ahead_low, from_hist, from_up, inv_mixed, inv_back, inv_lags, weave, unweave,
     out_se, out_mr, out_short, out_medium,
     se_behind, mr_behind, se_after, mr_after, cot_after,
-    win, y1, q1, k1, v1, pse, z1, k2, v2, z2,
-    hist, up, kspec, gspec, xspec, damp,
+    win, y1, q1, k1, v1, pse, z1, k2, v2, z2, upstream,
+    hist_in, hist_out, up_in, up_out, product, raised, inner, alive, outgoing, kspec, gspec, xspec, damp,
     dwide, d2, dz1, d1,
     dks, rs, ag, sks, srs, sag,
     edge_send, edge_recv, hist_send, hist_recv, up_send, up_recv,
@@ -67,7 +76,7 @@
     lane_width = channels // lane_blocks
     piece_rows = taps // row_blocks
     per_group = group // lane_width
-    end = rows + EDGE
+    wide = rows + 2 * EDGE
     up_rows = taps + EDGE
     me = lax.axis_index("ctx")
     has_behind = me > 0
@@ -112,14 +121,14 @@
     def hist_copy(i):
         cols = pl.ds(pl.multiple_of(i * group, group), group)
         return remote(
-            hist.at[pl.ds(rows, taps), cols], hist.at[pl.ds(0, taps), cols],
+            hist_out.at[:, cols], hist_in.at[:, cols],
             hist_send.at[i], hist_recv.at[i], me + 1,
         )
 
     def up_copy(i):
         cols = pl.ds(pl.multiple_of(i * group, group), group)
         return remote(
-            up.at[pl.ds(0, up_rows), cols], up.at[pl.ds(rows, up_rows), cols],
+            up_out.at[:, cols], up_in.at[pl.ds(0, up_rows), cols],
             up_send.at[i], up_recv.at[i], me - 1,
         )
 
@@ -137,25 +146,24 @@
     def _():
         se_behind[...] = jnp.zeros_like(se_behind)
         mr_behind[...] = jnp.zeros_like(mr_behind)
-        hist[0:taps, :] = jnp.zeros((taps, channels), BF16)
+        hist_in[...] = jnp.zeros_like(hist_in)
 
     @pl.when(jnp.logical_not(has_after))
     def _():
         se_after[...] = jnp.zeros_like(se_after)
         mr_after[...] = jnp.zeros_like(mr_after)
         cot_after[...] = jnp.zeros_like(cot_after)
-        up[rows : rows + up_rows, :] = jnp.zeros((up_rows, channels), BF16)
-
-    spare = length - (taps + rows + EDGE)
+        up_in[0:up_rows, :] = jnp.zeros((up_rows, channels), BF16)
+
+    spare = length - rows - up_rows
     if spare:
-        hist[length - spare :, :] = jnp.zeros((spare, channels), BF16)
-        up[length - spare :, :] = jnp.zeros((spare, channels), BF16)
-    win[:, 0:PAD, :] = jnp.zeros((5, PAD, group), F32)
-    y1[0:PAD, :] = jnp.zeros((PAD, group), F32)
-    pse[0:PAD, :] = jnp.zeros((PAD, channels), F32)
-    d2[:, end:, :] = jnp.zeros((3, d2.shape[1] - end, group), F32)
-    dz1[end:, :] = jnp.zeros((dz1.shape[0] - end, group), F32)
+        up_in[up_rows:, :] = jnp.zeros((spare, channels), BF16)
     sks[...] = jnp.zeros_like(sks)
+    at_row = lax.broadcasted_iota(jnp.int32, (wide, group), 0)
+    placed = lax.rem(at_row, 8) * (wide // 8) + at_row // 8
+    inside = jnp.where(has_after, 1.0, 0.0).astype(F32)
+    inner[...] = jnp.where((placed >= EDGE) & (placed < EDGE + rows), 1.0, 0.0).astype(F32)
+    alive[...] = jnp.where(placed >= EDGE + rows, inside, 1.0).astype(F32)
 
     def spectra(i, carry):
         cols = pl.ds(pl.multiple_of(i * group, group), group)
@@ -187,45 +195,54 @@
 
     def forward(i, carry):
         cols = pl.ds(pl.multiple_of(i * group, group), group)
+        blank = jnp.zeros((EDGE, group), BF16)
+
+        def woven(*pieces):
+            return jnp.dot(weave[...], jnp.concatenate(pieces, axis=0), preferred_element_type=F32)
+
         for part in range(3):
-            win[part, PAD : PAD + EDGE, :] = se_behind[part, :, cols].astype(F32)
-            win[part, PAD + EDGE : PAD + EDGE + rows, :] = se[part, :, cols].astype(F32)
-            win[part, PAD + EDGE + rows :, :] = se_after[part, :, cols].astype(F32)
-        for part in range(2):
-            win[3 + part, PAD : PAD + EDGE, :] = mr_behind[part, :, cols].astype(F32)
-            win[3 + part, PAD + EDGE : PAD + EDGE + rows, :] = mr[part, :, cols].astype(F32)
-        win[4, PAD + EDGE + rows :, :] = mr_after[:, cols].astype(F32)
+            win[part, NEAR:, :] = woven(se_behind[part, :, cols], se[part, :, cols], se_after[part, :, cols])
+        win[3, NEAR:, :] = woven(mr_behind[0, :, cols], mr[0, :, cols], blank)
+        win[4, NEAR:, :] = woven(mr_behind[1, :, cols], mr[1, :, cols], mr_after[:, cols])
+        upstream[:, cols] = woven(blank, cot[:, cols], cot_after[:, cols])
+        for part in range(5):
+            win[part, 0:NEAR, :] = win[part, wide - 1 : wide + NEAR - 1, :]
 
         def se_mix(part, at, size):
             return sum(
-                sef[3 * j + part : 3 * j + part + 1, cols] * win[part, pl.ds(PAD + at - j, size), :]
+                sef[j, part : part + 1, cols] * win[part, pl.ds(NEAR + at - 8 * j, size), :]
                 for j in range(feat)
             )
 
-        for at, size in [(0, EDGE)] + chunks(EDGE, EDGE + end, 32):
-            here = pl.ds(PAD + at, size)
-            q = se_mix(0, at, size)
+        for at, size in chunks(0, wide, 32):
+            here = pl.ds(at, size)
             k = se_mix(1, at, size)
             v = se_mix(2, at, size)
-            q1[here, cols] = q
+            q1[here, cols] = se_mix(0, at, size)
             k1[here, cols] = k
             v1[here, cols] = v
-            pse[here, cols] = (k * v).astype(BF16).astype(F32)
+            pse[pl.ds(FAR + at, size), cols] = (k * v).astype(BF16).astype(F32)
+        pse[0:FAR, cols] = pse[wide - 1 : wide + FAR - 1, cols]
+
+        for at, size in chunks(0, wide, 32):
+            here = pl.ds(at, size)
             z = sum(
-                sfilt[j : j + 1, cols] * pse[pl.ds(PAD + at - j, size), cols] for j in range(short)
+                sfilt[j : j + 1, cols] * pse[pl.ds(FAR + at - 8 * j, size), cols] for j in range(short)
             )
             z1[here, cols] = z
-            y1[here, :] = (q * z).astype(BF16).astype(F32)
-            if at < EDGE:
-                continue
+            y1[pl.ds(NEAR + at, size), :] = (q1[here, cols] * z).astype(BF16).astype(F32)
+        y1[0:NEAR, :] = y1[wide - 1 : wide + NEAR - 1, :]
+
+        for at, size in chunks(0, wide, 32):
+            here = pl.ds(at, size)
 
             def mr_mix(part):
                 return sum(
-                    mrf[3 * j + part : 3 * j + part + 1, cols]
+                    mrf[j, part : part + 1, cols]
                     * (
-                        y1[pl.ds(PAD + at - j, size), :]
+                        y1[pl.ds(NEAR + at - 8 * j, size), :]
                         if part == 2
-                        else win[3 + part, pl.ds(PAD + at - j, size), :]
+                        else win[3 + part, pl.ds(NEAR + at - 8 * j, size), :]
                     )
                     for j in range(feat)
                 )
@@ -234,10 +251,15 @@
             v = mr_mix(2)
             k2[here, cols] = k
             v2[here, cols] = v
-            t = at - EDGE
-            hist[pl.ds(taps + t, size), cols] = (k * v).astype(BF16)
-            if t < rows:
-                up[pl.ds(t, size), cols] = (cot[pl.ds(t, size), cols].astype(F32) * mr_mix(0)).astype(BF16)
+            product[here, :] = (k * v).astype(BF16)
+            raised[here, :] = (upstream[here, cols] * mr_mix(0)).astype(BF16)
+
+        hist_out[:, cols] = jnp.dot(
+            unweave[rows - taps : rows, :], product[...], preferred_element_type=F32
+        ).astype(BF16)
+        up_out[:, cols] = jnp.dot(
+            unweave[0:up_rows, :], raised[...], preferred_element_type=F32
+        ).astype(BF16)
 
         @pl.when(has_after)
         def _():
@@ -247,10 +269,8 @@
         def _():
             up_copy(i).start()
 
-        gspec[:, cols] = jnp.dot(ahead[:, 0:rows], up[0:rows, cols], preferred_element_type=F32)
-        xspec[:, cols] = jnp.dot(
-            ahead[:, taps:length], hist[taps:length, cols], preferred_element_type=F32
-        )
+        gspec[:, cols] = jnp.dot(from_up[...], raised[...], preferred_element_type=F32)
+        xspec[:, cols] = jnp.dot(from_hist[...], product[...], preferred_element_type=F32)
         return carry
 
     lax.fori_loop(0, groups, forward, 0)
@@ -288,7 +308,7 @@
         def _():
             hist_copy(i).wait_recv()
 
-        x = xspec[:, cols] + jnp.dot(ahead[:, 0:taps], hist[0:taps, cols], preferred_element_type=F32)
+        x = xspec[:, cols] + jnp.dot(ahead[:, 0:taps], hist_in[:, cols], preferred_element_type=F32)
         xr, xi = x[:half], x[half:]
         gr, gi = gspec[0:half, cols], gspec[half:, cols]
         lag = jnp.concatenate(
@@ -313,8 +333,6 @@
 
     lax.fori_loop(0, groups, medium, 0)
 
-    inside = jnp.where(has_after, 1.0, 0.0).astype(F32)
-
     def backward(i, carry):
         cols = pl.ds(pl.multiple_of(i * group, group), group)
 
@@ -323,7 +341,7 @@
             up_copy(i).wait_recv()
 
         d = gspec[:, cols] + jnp.dot(
-            ahead[:, rows:length], up[rows:length, cols], preferred_element_type=F32
+            ahead[:, rows:length], up_in[:, cols], preferred_element_type=F32
         )
         dr, di = d[:half], d[half:]
         kr, ki = kspec[0:half, cols], kspec[half:, cols]
@@ -332,58 +350,59 @@
         )
         dwide[...] = jnp.dot(inv_back[...], y, preferred_element_type=F32)
 
-        for t, size in chunks(0, end, 32):
+        for t, size in chunks(0, wide, 32):
             here = pl.ds(t, size)
-            there = pl.ds(PAD + EDGE + t, size)
-            w = dwide[here, :]
-            if t >= rows:
-                w = w * inside
-                g = cot_after[:, cols].astype(F32)
-            else:
-                g = cot[here, cols].astype(F32)
-            d2[0, here, :] = g * z2[here, cols]
-            d2[1, here, :] = w * v2[there, cols]
-            d2[2, here, :] = w * k2[there, cols]
+            w = dwide[here, :] * alive[here, :]
+            d2[0, here, :] = upstream[here, cols] * z2[here, cols]
+            d2[1, here, :] = w * v2[here, cols]
+            d2[2, here, :] = w * k2[here, cols]
+        for part in range(3):
+            d2[part, wide:, :] = d2[part, 1 : NEAR + 1, :]
 
         def mr_back(part, t, size):
             return sum(
-                mrf[3 * j + part : 3 * j + part + 1, cols] * d2[part, pl.ds(t + j, size), :]
+                mrf[j, part : part + 1, cols] * d2[part, pl.ds(t + 8 * j, size), :]
                 for j in range(feat)
             )
 
-        for t, size in chunks(0, end, 32):
+        for t, size in chunks(0, wide, 32):
             here = pl.ds(t, size)
-            there = pl.ds(PAD + EDGE + t, size)
             dy = mr_back(2, t, size)
-            d1[0, here, :] = dy * z1[there, cols]
-            dz1[here, :] = dy * q1[there, cols]
-            if t < rows:
-                out_mr[0, here, cols] = mr_back(0, t, size).astype(BF16)
-                out_mr[1, here, cols] = mr_back(1, t, size).astype(BF16)
+            d1[0, here, :] = dy * z1[here, cols]
+            dz1[here, :] = dy * q1[here, cols]
+            outgoing[0, here, :] = mr_back(0, t, size).astype(BF16)
+            outgoing[1, here, :] = mr_back(1, t, size).astype(BF16)
+        dz1[wide:, :] = dz1[1 : FAR + 1, :]
+        for part in range(2):
+            out_mr[part, :, cols] = jnp.dot(
+                unweave[...], outgoing[part], preferred_element_type=F32
+            ).astype(BF16)
 
         sums = [jnp.zeros((8, group), F32) for _ in range(short)]
-        for t, size in chunks(0, end, 32):
+        for t, size in chunks(0, wide, 32):
             here = pl.ds(t, size)
-            there = pl.ds(PAD + EDGE + t, size)
-            w = sum(sfilt[j : j + 1, cols] * dz1[pl.ds(t + j, size), :] for j in range(short))
-            d1[1, here, :] = w * v1[there, cols]
-            d1[2, here, :] = w * k1[there, cols]
-            if t < rows:
-                dz = dz1[here, :]
-                for j in range(short):
-                    term = dz * pse[pl.ds(PAD + EDGE + t - j, size), cols]
-                    for s in range(0, size, 8):
-                        sums[j] = sums[j] + term[s : s + 8]
+            w = sum(sfilt[j : j + 1, cols] * dz1[pl.ds(t + 8 * j, size), :] for j in range(short))
+            d1[1, here, :] = w * v1[here, cols]
+            d1[2, here, :] = w * k1[here, cols]
+            dz = dz1[here, :] * inner[here, :]
+            for j in range(short):
+                term = dz * pse[pl.ds(FAR + t - 8 * j, size), cols]
+                for s in range(0, size, 8):
+                    sums[j] = sums[j] + term[s : s + 8]
         for j in range(short):
             sks[j : j + 1, cols] = jnp.sum(sums[j], axis=0, keepdims=True)
-
-        for t, size in chunks(0, rows, 32):
-            here = pl.ds(t, size)
-            for part in range(3):
-                out_se[part, here, cols] = sum(
-                    sef[3 * j + part : 3 * j + part + 1, cols] * d1[part, pl.ds(t + j, size), :]
+        for part in range(3):
+            d1[part, wide:, :] = d1[part, 1 : NEAR + 1, :]
+
+        for part in range(3):
+            for t, size in chunks(0, wide, 32):
+                outgoing[2 + part, pl.ds(t, size), :] = sum(
+                    sef[j, part : part + 1, cols] * d1[part, pl.ds(t + 8 * j, size), :]
                     for j in range(feat)
                 ).astype(BF16)
+            out_se[part, :, cols] = jnp.dot(
+                unweave[...], outgoing[2 + part], preferred_element_type=F32
+            ).astype(BF16)
 
         @pl.when(i == max(groups - 2, 0))
         def _():
@@ -446,25 +465,29 @@
     taps, short, feat = mr_filter.shape[0], se_filter.shape[0], se_featurizer.shape[0]
     group = min(256, channels)
     groups = channels // group
-    length, ahead, ahead_low, inv_mixed, inv_back, inv_lags = transforms(rows, taps)
+    length, tables = transforms(rows, taps)
     lane_blocks = min(n_ctx, 8)
     lane_width = channels // lane_blocks
     piece_rows = taps // (n_ctx // lane_blocks)
-    wide = PAD + EDGE + rows + EDGE
-    end = rows + EDGE
+    wide = rows + 2 * EDGE
     vmem = pltpu.VMEM
     dma = pltpu.SemaphoreType.DMA
     scratch = (
         [vmem((3, EDGE, channels), BF16), vmem((2, EDGE, channels), BF16)]
         + [vmem((3, EDGE, channels), BF16), vmem((EDGE, channels), BF16), vmem((EDGE, channels), BF16)]
-        + [vmem((5, wide, group), F32), vmem((wide, group), F32)]
-        + [vmem((wide, channels), F32)] * 7
-        + [vmem((end, channels), F32)]
-        + [vmem((length, channels), BF16)] * 2
+        + [vmem((5, NEAR + wide, group), F32), vmem((NEAR + wide, group), F32)]
+        + [vmem((wide, channels), F32)] * 3
+        + [vmem((FAR + wide, channels), F32)]
+        + [vmem((wide, channels), F32)] * 5
+        + [vmem((taps, channels), BF16)] * 2
+        + [vmem((length - rows, channels), BF16), vmem((taps + EDGE, channels), BF16)]
+        + [vmem((wide, group), BF16)] * 2
+        + [vmem((wide, group), F32)] * 2
+        + [vmem((5, wide, group), BF16)]
         + [vmem((length, channels), F32)] * 3
         + [vmem((taps, channels), F32)]
-        + [vmem((end, group), F32), vmem((3, end + 16, group), F32)]
-        + [vmem((end + 16, group), F32), vmem((3, end + 16, group), F32)]
+        + [vmem((wide, group), F32), vmem((3, wide + NEAR, group), F32)]
+        + [vmem((wide + FAR, group), F32), vmem((3, wide + NEAR, group), F32)]
         + [vmem((taps, channels), BF16)]
         + [vmem((n_ctx, piece_rows, lane_width), BF16)] * 2
         + [vmem((8, channels), F32)]
@@ -481,7 +504,7 @@
             jax.ShapeDtypeStruct((short, channels), F32),
             jax.ShapeDtypeStruct((taps, channels), F32),
         ),
-        in_specs=[pl.BlockSpec(memory_space=pltpu.VMEM)] * 13,
+        in_specs=[pl.BlockSpec(memory_space=pltpu.VMEM)] * (8 + len(tables)),
         out_specs=[pl.BlockSpec(memory_space=pltpu.VMEM)] * 4,
         scratch_shapes=scratch,
         compiler_params=pltpu.CompilerParams(
@@ -495,12 +518,12 @@
         jnp.transpose(se_input, (1, 0, 2)),
         jnp.transpose(mr_input, (1, 0, 2)),
         cotangent,
-        se_featurizer.reshape(3 * feat, channels),
-        mr_featurizer.reshape(3 * feat, channels),
+        se_featurizer,
+        mr_featurizer,
         se_filter,
         mr_filter,
         decay_rate[None, :],
-        ahead, ahead_low, inv_mixed, inv_back, inv_lags,
+        *tables,
     )
     return jnp.transpose(out_se, (1, 0, 2)), jnp.transpose(out_mr, (1, 0, 2)), out_short, out_medium
 

time: 65.5 us -> 61.6 us (0.940)
  local copies, waits for them, and re-layouts: 11.3 us -> 8.42 us
  Pallas kernels: 53.2 us -> 52.4 us
    reshape x2 -> x0, local copies, waits for them, and re-layouts: 2.89 us -> none  [the longest x1 1.45 us: local(): se_featurizer.reshape(3 * feat, channels)]
    pallas_call x1, Pallas kernels: 53.2 us -> 52.4 us  [local(): pl.pallas_call(functools.partial(body, n_ctx, length, taps, short, feat,...]
where the time goes in v1:
time: 61.6 us; the launch traced here: 61.5 us
  Pallas kernels  52.4 us (85%)
  local copies, waits for them, and re-layouts  8.42 us (14%)
  between operations  0.65 us (1%)
    pallas_call x1, Pallas kernels, local(): pl.pallas_call(functools.partial(body, n_ctx, length, taps, short, feat,...  52.4 us
    unnamed x11, local copies, waits for them, and re-layouts  8.42 us

profile of v1, /device:TPU:0, one launch (start us, length us, event | category | flops | bytes accessed | tf_op | source)
XLA Modules:
  0.0 61.5 jit_solution(2399470702030955061)
XLA Ops:
  0.6 2.5 %copy.24 = bf16[256,2,1024]{2,0,1:T(8,128)(2,1)} copy(bf16[256,2,1024]{2,1,0:T(2,128)(2,1)} %param.18) | data formatting | bytes 2097152 | tf_op args[1]
  3.1 52.4 %hyena_pair.1 = (bf16[3,256,1024]{2,1,0:T(8,128)(2,1)}, bf16[2,256,1024]{2,1,0:T(8,128)(2,1)}, f32[7,1024]{1,0:T(8,128)}, f32[128,1024]{1,0:T(8,128)}) custom-call(bf16[3,256,1024]{2,1,0:T(8,128)(2,1)} %bitcast.10, bf16[2,256,1024]{2,1,0:T(8,128)(2,1)} %bitcast.9, bf16[256,1024]{1,0:T(8,128)(2,1)} %cot.1, f32[3,3,1024]{2,1,0:T(4,128)} %sef.1, ...), custom_call_target="tpu_custom_call" | custom-call | flops 2126512128 | bytes 7340032 | tf_op jit(solution)/shard_map/hyena_pair/pallas_call | solution.py:499
  55.5 0.0 copy-start
  55.5 3.4 %copy.22 = bf16[256,2,1024]{2,1,0:T(2,128)(2,1)} copy(bf16[256,2,1024]{2,0,1:T(8,128)(2,1)} %bitcast.8) | data formatting | bytes 2097152
  58.9 0.0 copy-done
  58.9 0.0 copy-start.2
  58.9 0.0 copy-start.1
  58.9 1.1 %copy.28 = bf16[256,3,1024]{2,0,1:T(8,128)(2,1)} copy(bf16[256,3,1024]{2,0,1:T(8,128)(2,1)S(1)} %bitcast.7) | data formatting | bytes 3145728
  60.0 0.0 copy-done.2
  60.0 0.6 %copy.29 = f32[7,1024]{1,0:T(8,128)} copy(f32[7,1024]{1,0:T(8,128)S(1)} %copy-done.2) | data formatting | bytes 57344
  60.7 0.0 copy-done.1
  60.7 0.8 %copy.30 = f32[128,1024]{1,0:T(8,128)} copy(f32[128,1024]{1,0:T(8,128)S(1)} %copy-done.1) | data formatting | bytes 1048576
Async XLA Ops:
  55.5 3.4 %copy-start = (bf16[3,256,1024]{2,1,0:T(8,128)(2,1)S(1)}, bf16[3,256,1024]{2,1,0:T(8,128)(2,1)}, u32[]{:S(2)}) copy-start(bf16[3,256,1024]{2,1,0:T(8,128)(2,1)} %get-tuple-element.8) | copy-start | bytes 4718596
  58.9 1.1 %copy-start.2 = (f32[7,1024]{1,0:T(8,128)S(1)}, f32[7,1024]{1,0:T(8,128)}, u32[]{:S(2)}) copy-start(f32[7,1024]{1,0:T(8,128)} %get-tuple-element.22) | copy-start | bytes 86020
  58.9 1.8 %copy-start.1 = (f32[128,1024]{1,0:T(8,128)S(1)}, f32[128,1024]{1,0:T(8,128)}, u32[]{:S(2)}) copy-start(f32[128,1024]{1,0:T(8,128)} %get-tuple-element.23) | copy-start | bytes 1572868

commit v2 on v1

--- a/solution.py
+++ b/solution.py
@@ -58,7 +58,8 @@
 
 def body(
     n_ctx, length, taps, short, feat, group,
-    se, mr, cot, sef, mrf, sfilt, mfilt, decay, ahead, ahead_low, from_hist, from_up, inv_mixed, inv_back, inv_lags, weave, unweave,
+    se_far, mr_far, cot_far, sef, mrf, sfilt, mfilt, decay, ahead, ahead_low,
+    from_hist_far, from_up_far, inv_mixed_far, inv_back_far, inv_lags_far, weave_far, unweave_far,
     out_se, out_mr, out_short, out_medium,
     se_behind, mr_behind, se_after, mr_after, cot_after,
     win, y1, q1, k1, v1, pse, z1, k2, v2, z2, upstream,
@@ -67,8 +68,9 @@
     dks, rs, ag, sks, srs, sag,
     edge_send, edge_recv, hist_send, hist_recv, up_send, up_recv,
     rs_send, rs_recv, ag_send, ag_recv, srs_send, srs_recv, sag_send, sag_recv,
+    se, mr, cot, from_hist, from_up, inv_mixed, inv_back, inv_lags, weave, unweave, load_sem,
 ):
-    rows, channels = cot.shape
+    rows, channels = cot_far.shape
     half = length // 2
     groups = channels // group
     lane_blocks = min(n_ctx, 8)
@@ -82,6 +84,18 @@
     has_behind = me > 0
     has_after = me < n_ctx - 1
 
+    far = (
+        se_far, mr_far, cot_far, weave_far, from_hist_far, from_up_far, unweave_far,
+        inv_lags_far, inv_mixed_far, inv_back_far,
+    )
+    close = (se, mr, cot, weave, from_hist, from_up, unweave, inv_lags, inv_mixed, inv_back)
+    loads = [
+        pltpu.make_async_copy(src, dst, load_sem.at[at])
+        for at, (src, dst) in enumerate(zip(far, close))
+    ]
+    for load in loads:
+        load.start()
+
     barrier = pltpu.get_barrier_semaphore()
 
     def greet(step, carry):
@@ -103,19 +117,29 @@
     last = pl.ds(rows - EDGE, EDGE)
     first = pl.ds(0, EDGE)
 
-    def to_after():
+    def to_after(i):
         to = me + 1
+        cols = pl.ds(pl.multiple_of(i * group, group), group)
+        pairs = [
+            (se_far.at[:, last, cols], se_behind.at[:, :, cols]),
+            (mr_far.at[:, last, cols], mr_behind.at[:, :, cols]),
+        ]
         return [
-            remote(se.at[:, last, :], se_behind, edge_send.at[0], edge_recv.at[0], to),
-            remote(mr.at[:, last, :], mr_behind, edge_send.at[1], edge_recv.at[1], to),
+            remote(src, dst, edge_send.at[at, i], edge_recv.at[at, i], to)
+            for at, (src, dst) in enumerate(pairs)
         ]
 
-    def to_behind():
+    def to_behind(i):
         to = me - 1
+        cols = pl.ds(pl.multiple_of(i * group, group), group)
+        pairs = [
+            (se_far.at[:, first, cols], se_after.at[:, :, cols]),
+            (mr_far.at[1, first, cols], mr_after.at[:, cols]),
+            (cot_far.at[first, cols], cot_after.at[:, cols]),
+        ]
         return [
-            remote(se.at[:, first, :], se_after, edge_send.at[2], edge_recv.at[2], to),
-            remote(mr.at[1, first, :], mr_after, edge_send.at[3], edge_recv.at[3], to),
-            remote(cot.at[first, :], cot_after, edge_send.at[4], edge_recv.at[4], to),
+            remote(src, dst, edge_send.at[2 + at, i], edge_recv.at[2 + at, i], to)
+            for at, (src, dst) in enumerate(pairs)
         ]
 
     def hist_copy(i):
@@ -132,15 +156,17 @@
             up_send.at[i], up_recv.at[i], me - 1,
         )
 
-    @pl.when(has_after)
-    def _():
-        for copy in to_after():
-            copy.start()
-
-    @pl.when(has_behind)
-    def _():
-        for copy in to_behind():
-            copy.start()
+    for i in range(groups):
+
+        @pl.when(has_after)
+        def _():
+            for copy in to_after(i):
+                copy.start()
+
+        @pl.when(has_behind)
+        def _():
+            for copy in to_behind(i):
+                copy.start()
 
     @pl.when(jnp.logical_not(has_behind))
     def _():
@@ -183,18 +209,22 @@
 
     lax.fori_loop(0, groups, spectra, 0)
 
-    @pl.when(has_behind)
-    def _():
-        for copy in to_after():
-            copy.wait_recv()
-
-    @pl.when(has_after)
-    def _():
-        for copy in to_behind():
-            copy.wait_recv()
+    for load in loads:
+        load.wait()
 
     def forward(i, carry):
         cols = pl.ds(pl.multiple_of(i * group, group), group)
+
+        @pl.when(has_behind)
+        def _():
+            for copy in to_after(i):
+                copy.wait_recv()
+
+        @pl.when(has_after)
+        def _():
+            for copy in to_behind(i):
+                copy.wait_recv()
+
         blank = jnp.zeros((EDGE, group), BF16)
 
         def woven(*pieces):
@@ -438,16 +468,16 @@
 
     @pl.when(has_after)
     def _():
-        for copy in to_after():
-            copy.wait_send()
         for i in range(groups):
+            for copy in to_after(i):
+                copy.wait_send()
             hist_copy(i).wait_send()
 
     @pl.when(has_behind)
     def _():
-        for copy in to_behind():
-            copy.wait_send()
         for i in range(groups):
+            for copy in to_behind(i):
+                copy.wait_send()
             up_copy(i).wait_send()
 
     for_peers(lambda d: rs_copy(d, me).wait_send())
@@ -492,9 +522,12 @@
         + [vmem((n_ctx, piece_rows, lane_width), BF16)] * 2
         + [vmem((8, channels), F32)]
         + [vmem((n_ctx, 8, lane_width), F32)] * 2
-        + [dma((5,))] * 2
+        + [dma((5, groups))] * 2
         + [dma((groups,))] * 4
         + [dma((n_ctx,))] * 8
+        + [vmem((3, rows, channels), BF16), vmem((2, rows, channels), BF16), vmem((rows, channels), BF16)]
+        + [vmem(table.shape, BF16) for table in tables[2:]]
+        + [dma((10,))]
     )
     out_se, out_mr, out_short, out_medium = pl.pallas_call(
         functools.partial(body, n_ctx, length, taps, short, feat, group),
@@ -504,7 +537,9 @@
             jax.ShapeDtypeStruct((short, channels), F32),
             jax.ShapeDtypeStruct((taps, channels), F32),
         ),
-        in_specs=[pl.BlockSpec(memory_space=pltpu.VMEM)] * (8 + len(tables)),
+        in_specs=[pl.BlockSpec(memory_space=pl.ANY)] * 3
+        + [pl.BlockSpec(memory_space=pltpu.VMEM)] * 7
+        + [pl.BlockSpec(memory_space=pl.ANY)] * 7,
         out_specs=[pl.BlockSpec(memory_space=pltpu.VMEM)] * 4,
         scratch_shapes=scratch,
         compiler_params=pltpu.CompilerParams(

time: 61.6 us -> 59.4 us (0.964)
  Pallas kernels: 52.4 us -> 50.1 us
    pallas_call x1, Pallas kernels: 52.4 us -> 50.1 us  [local(): pl.pallas_call(functools.partial(body, n_ctx, length, taps, short, feat,...]
where the time goes in v2:
time: 59.4 us; the launch traced here: 59.2 us
  Pallas kernels  50.1 us (84%)
  local copies, waits for them, and re-layouts  8.42 us (14%)
  between operations  0.65 us (1%)
    pallas_call x1, Pallas kernels, local(): pl.pallas_call(functools.partial(body, n_ctx, length, taps, short, feat,...  50.1 us
    unnamed x11, local copies, waits for them, and re-layouts  8.42 us

profile of v2, /device:TPU:0, one launch (start us, length us, event | category | flops | bytes accessed | tf_op | source)
XLA Modules:
  0.0 59.2 jit_solution(11247751690500440329)
XLA Ops:
  0.6 2.5 %copy.24 = bf16[256,2,1024]{2,0,1:T(8,128)(2,1)} copy(bf16[256,2,1024]{2,1,0:T(2,128)(2,1)} %param.18) | data formatting | bytes 2097152 | tf_op args[1]
  3.1 50.1 %hyena_pair.1 = (bf16[3,256,1024]{2,1,0:T(8,128)(2,1)}, bf16[2,256,1024]{2,1,0:T(8,128)(2,1)}, f32[7,1024]{1,0:T(8,128)}, f32[128,1024]{1,0:T(8,128)}) custom-call(bf16[3,256,1024]{2,1,0:T(8,128)(2,1)} %bitcast.10, bf16[2,256,1024]{2,1,0:T(8,128)(2,1)} %bitcast.9, bf16[256,1024]{1,0:T(8,128)(2,1)} %cot_far.1, f32[3,3,1024]{2,1,0:T(4,128)} %sef.1, ...), custom_call_target="tpu_custom_call" | custom-call | flops 2126512128 | bytes 7340032 | tf_op jit(solution)/shard_map/hyena_pair/pallas_call | solution.py:532
  53.2 0.0 copy-start
  53.2 3.4 %copy.22 = bf16[256,2,1024]{2,1,0:T(2,128)(2,1)} copy(bf16[256,2,1024]{2,0,1:T(8,128)(2,1)} %bitcast.8) | data formatting | bytes 2097152
  56.6 0.0 copy-done
  56.6 0.0 copy-start.2
  56.6 0.0 copy-start.1
  56.6 1.1 %copy.28 = bf16[256,3,1024]{2,0,1:T(8,128)(2,1)} copy(bf16[256,3,1024]{2,0,1:T(8,128)(2,1)S(1)} %bitcast.7) | data formatting | bytes 3145728
  57.8 0.0 copy-done.2
  57.8 0.6 %copy.29 = f32[7,1024]{1,0:T(8,128)} copy(f32[7,1024]{1,0:T(8,128)S(1)} %copy-done.2) | data formatting | bytes 57344
  58.4 0.0 copy-done.1
  58.4 0.8 %copy.30 = f32[128,1024]{1,0:T(8,128)} copy(f32[128,1024]{1,0:T(8,128)S(1)} %copy-done.1) | data formatting | bytes 1048576
Async XLA Ops:
  53.2 3.4 %copy-start = (bf16[3,256,1024]{2,1,0:T(8,128)(2,1)S(1)}, bf16[3,256,1024]{2,1,0:T(8,128)(2,1)}, u32[]{:S(2)}) copy-start(bf16[3,256,1024]{2,1,0:T(8,128)(2,1)} %get-tuple-element.8) | copy-start | bytes 4718596
  56.6 1.1 %copy-start.2 = (f32[7,1024]{1,0:T(8,128)S(1)}, f32[7,1024]{1,0:T(8,128)}, u32[]{:S(2)}) copy-start(f32[7,1024]{1,0:T(8,128)} %get-tuple-element.22) | copy-start | bytes 86020
  56.6 1.8 %copy-start.1 = (f32[128,1024]{1,0:T(8,128)S(1)}, f32[128,1024]{1,0:T(8,128)}, u32[]{:S(2)}) copy-start(f32[128,1024]{1,0:T(8,128)} %get-tuple-element.23) | copy-start | bytes 1572868
